TPU v7x, 32 devices: a whole 2x2x4 slice. The times are simulated.
32 devices in a mesh: wall: 4 (over y, x), drops: 8 (over z, core).
Axes of the slice: x: 2, y: 2, z: 4, core: 2. Of those that a mesh axis runs over, the one named last changes fastest.
Arguments:
- drop_points: float32 [256, 3, 544], P(('wall', 'drops')), may hold values from -6 to 6
- drop_strength: float32 [256, 3, 544], P(('wall', 'drops')), may hold values from -0.25 to 0.25
- upsample: float32 [544, 2112], replicated, may hold values from -0.25 to 0.25
- base_velocity: float32 [256, 3, 544], P(('wall', 'drops')), may hold values from -6 to 6
- near_drops: int32 [256, 4], P(('wall', 'drops')), may hold values from 0 to 255, as said below
- near_count: int32 [256], P(('wall', 'drops')), may hold values from 2 to 4
- patch_points: float32 [8192, 192], P('wall'), may hold values from -6 to 6
- patch_strength: float32 [8192, 192], P('wall'), may hold values from -1 to 1
- wall_near: int32 [256, 8], P(('wall', 'drops')), may hold values from 0 to 8191
Outputs:
- drop_velocity: float32 [256, 3, 544], P(('wall', 'drops'))
Inputs may be any that keep to these rules, and one draw needn't show every extreme that they name: `near_drops`: each entry names a drop of the same drop group (same index along wall). Of the 32 entries of one device, at most 4 name drops of any one device of the group, and on every device some device of the group is named exactly 4 times. Entries at slots k >= near_count are ignored.
All inputs are finite; a program needn't handle non-finite values.
Results may differ from a plain program's by a relative error of at most 0.0003.
Values sent between devices are 32-bit elements; how exact they have to be, the bound alone decides.
A program may use at most 128 MiB of HBM per device.

v0:
```python
import functools

import jax
import jax.numpy as jnp
from jax import lax
from jax.experimental import pallas as pl
from jax.experimental.pallas import tpu as pltpu
from jax.sharding import PartitionSpec as P

BF, F32 = jnp.bfloat16, jnp.float32
CHUNK = 512
GROUP = 16


def kernel_pieces(value):
    first = value.astype(BF).astype(F32)
    rest = value - first
    second = rest.astype(BF).astype(F32)
    return first, second, (rest - second).astype(BF).astype(F32)


def target_features(packed):
    row = lax.broadcasted_iota(jnp.int32, packed.shape, 0)
    scaled = jnp.where((row >= 3) & (row < 6), 2.0 * packed, 0.0)
    norm = jnp.sum(scaled * scaled, axis=0, keepdims=True) + 1.0
    coords = kernel_pieces(-2.0 * scaled)
    norms = [jnp.where(row == 6, part, 0.0) for part in kernel_pieces(norm)]
    one = jnp.where(row == 7, 1.0, 0.0)
    blocks = [coords[0] + norms[0] + one, coords[1] + norms[1], coords[2] + norms[2]]
    blocks += [coords[0] + one, coords[1], coords[2], coords[0] + one, coords[1]]
    return jnp.concatenate(blocks, axis=0).T.astype(BF)


def pair_kernel(per_drop, counts, *refs):
    count = len(refs) - 17
    src, (scale, shift, tgt, base, out) = refs[:count], refs[count : count + 5]
    left, right, force, feat, acc_one, acc_cube = refs[count + 5 : count + 11]
    dist, high, low = (refs[k : k + 2] for k in range(count + 11, count + 17, 2))
    width = scale.shape[1]
    row = lax.broadcasted_iota(jnp.int32, (8, width), 0)

    nodes = feat.shape[0]
    starts = list(range(0, width, CHUNK))
    dims = (((1,), (1,)), ((), ()))

    def distances(n):
        size = min(CHUNK, width - starts[n])
        dist[n % 2][:, :size] = jnp.dot(
            feat[...], left[:, starts[n] : starts[n] + size], preferred_element_type=F32
        )

    def powers(n):
        size = min(CHUNK, width - starts[n])
        lanes = range(0, size, 128)
        weights = [
            [force[c : c + 1, starts[n] + lane : starts[n] + lane + 128] for c in range(3)]
            for lane in lanes
        ]
        for top in range(0, nodes, GROUP):
            rows = slice(top, min(top + GROUP, nodes))
            sums = [acc_one[c, rows] for c in range(3)]
            for weight, lane in zip(weights, lanes):
                inverse = lax.rsqrt(dist[n % 2][rows, lane : lane + 128])
                sums = [part + inverse * weight[c] for c, part in enumerate(sums)]
                cubed = inverse * inverse * inverse
                whole = cubed.astype(BF)
                high[n % 2][rows, lane : lane + 128] = whole
                low[n % 2][rows, lane : lane + 128] = (cubed - whole.astype(F32)).astype(BF)
            for c in range(3):
                acc_one[c, rows] = sums[c]

    def sums(n):
        size = min(CHUNK, width - starts[n])
        coefs = right[:, starts[n] : starts[n] + size]
        acc_cube[...] += lax.dot_general(
            high[n % 2][:, :size], coefs, dims, preferred_element_type=F32
        ) + lax.dot_general(low[n % 2][:, :size], coefs, dims, preferred_element_type=F32)

    def one_drop(i, _):
        acc_one[...] = jnp.zeros_like(acc_one)
        acc_cube[...] = jnp.zeros_like(acc_cube)
        own = tgt[i]
        feat[...] = target_features(own)

        def one_entry(k, _):
            rows = [ref[i * per_drop + k] for ref in src]
            filled = sum(ref.shape[2] for ref in src)
            if filled < width:
                rows.append(jnp.zeros((8, width - filled), F32))
            raw = jnp.concatenate(rows, axis=1) if len(rows) > 1 else rows[0]
            raw = raw * scale[...] + shift[...]
            square = raw * raw
            norm = square[3:4] + square[4:5] + square[5:6]
            values = jnp.where(row == 7, norm, raw)
            force[...] = values
            first, second, third = kernel_pieces(values)
            left[...] = jnp.concatenate(
                [first, first, first, second, second, second, third, third], axis=0
            ).astype(BF)
            cross = [values * raw[3 + c : 4 + c] for c in range(3)]
            along = cross[0][0:1] + cross[1][1:2] + cross[2][2:3]
            split = [kernel_pieces(part) for part in cross + [values * along]]
            parts = []
            for p, whole in enumerate((first, second, third)):
                parts += [whole] + [part[p] for part in split]
            parts.append(jnp.zeros_like(first))
            right[...] = jnp.concatenate(parts, axis=0).astype(BF)

            distances(0)
            for n in range(len(starts)):
                if n + 1 < len(starts):
                    distances(n + 1)
                powers(n)
                sums(n)
            return 0

        lax.fori_loop(0, counts[i], one_entry, 0)

        turned = acc_cube[...].T
        cube = turned[0:40] + turned[40:80] + turned[80:120]
        plain = [jnp.sum(acc_one[c].T, axis=0, keepdims=True) for c in range(3)]
        x = 2.0 * own[3:6]
        direct = cube[0:3]
        scalar = jnp.sum(x * direct, axis=0, keepdims=True) - (cube[8:9] + cube[17:18] + cube[26:27])
        total = base[i] + jnp.concatenate(plain, axis=0) + direct + cube[35:38] + x * scalar
        turned = [jnp.sum(x * cube[8 + 8 * c : 11 + 8 * c], axis=0, keepdims=True) for c in range(3)]
        out[i] = total - jnp.concatenate(turned, axis=0)
        return 0

    lax.fori_loop(0, out.shape[0], one_drop, 0)


def pair_sums(counts, src, scale, shift, tgt, base):
    drops, _, nodes = tgt.shape
    width = scale.shape[1]
    per_drop = src[0].shape[0] // drops
    pairs = drops * per_drop * nodes * width
    vmem = pl.BlockSpec(memory_space=pltpu.VMEM)
    return pl.pallas_call(
        functools.partial(pair_kernel, per_drop),
        out_shape=jax.ShapeDtypeStruct(base.shape, F32),
        in_specs=[pl.BlockSpec(memory_space=pltpu.SMEM)] + [vmem] * (len(src) + 4),
        out_specs=vmem,
        scratch_shapes=[
            pltpu.VMEM((64, width), BF),
            pltpu.VMEM((128, width), BF),
            pltpu.VMEM((8, width), F32),
            pltpu.VMEM((nodes, 64), BF),
            pltpu.VMEM((3, nodes, 128), F32),
            pltpu.VMEM((nodes, 128), F32),
        ]
        + [pltpu.VMEM((nodes, CHUNK), F32)] * 2
        + [pltpu.VMEM((nodes, CHUNK), BF)] * 4,
        compiler_params=pltpu.CompilerParams(vmem_limit_bytes=40 * 1024 * 1024),
        cost_estimate=pl.CostEstimate(
            flops=pairs * 4000, bytes_accessed=pairs // nodes * 32, transcendentals=pairs
        ),
    )(counts, *src, scale, shift, tgt, base)


def per_device(
    drop_points,
    drop_strength,
    upsample,
    base_velocity,
    near_drops,
    near_count,
    patch_points,
    patch_strength,
    wall_near,
):
    owned, _, coarse = drop_points.shape
    fine = upsample.shape[1]
    group = lax.axis_size("drops") * owned
    width = -(-(fine + coarse) // 128) * 128

    packed = jnp.concatenate(
        [drop_strength, drop_points, jnp.zeros((owned, 2, coarse), F32)], axis=1
    )
    spread = jnp.broadcast_to(packed[None], (group // owned,) + packed.shape)
    everyone = lax.all_to_all(spread, "drops", split_axis=0, concat_axis=0, tiled=True)
    everyone = everyone.reshape(group, 8, coarse)

    ranks = lax.axis_size("wall")
    held, patch_width = patch_points.shape
    listed = wall_near.shape[1]
    patch_nodes = patch_width // 3
    lists = jnp.broadcast_to(wall_near.reshape(1, owned * listed), (ranks, owned * listed))
    asked = lax.all_to_all(lists, "wall", split_axis=0, concat_axis=0, tiled=True).reshape(-1)
    mine = asked // held == lax.axis_index("wall")
    spot = jnp.where(mine, asked % held, 0)
    reply = jnp.concatenate(
        [jnp.take(patch_strength, spot, axis=0), jnp.take(patch_points, spot, axis=0)], axis=1
    )
    reply = jnp.where(mine[:, None], reply, 0.0)
    wall = lax.psum_scatter(reply, "wall", scatter_dimension=0, tiled=True)
    entries = jnp.take(everyone, near_drops.reshape(-1) % group, axis=0)
    upsampled = lax.dot_general(
        entries.reshape(-1, coarse),
        upsample,
        (((1,), (0,)), ((), ())),
        precision=lax.Precision.HIGH,
        preferred_element_type=F32,
    ).reshape(-1, 8, fine)

    def scale_of(lanes, plus):
        row = jnp.arange(8, dtype=jnp.int32)[:, None]
        lane = jnp.arange(lanes, dtype=jnp.int32)[None, :]
        sign = jnp.where((row < 3) & (lane >= plus), -2.0, 2.0)
        return jnp.where(row < 6, sign, 0.0).astype(F32), jnp.broadcast_to(
            (row == 6).astype(F32), (8, lanes)
        )

    near = pair_sums(
        near_count, (upsampled, entries), *scale_of(width, fine), packed, base_velocity
    )
    wall, near = lax.optimization_barrier((wall, near))
    wall = wall.reshape(owned, listed, 6, patch_nodes).transpose(0, 2, 1, 3)
    wall = wall.reshape(owned, 6, listed * patch_nodes)
    wall = jnp.concatenate([wall, jnp.zeros((owned, 2, listed * patch_nodes), F32)], axis=1)
    wall_width = listed * patch_nodes
    return pair_sums(
        jnp.ones((owned,), jnp.int32),
        (wall,),
        *scale_of(wall_width, wall_width),
        packed,
        near,
    )


def solution(mesh):
    return jax.shard_map(
        per_device,
        mesh=mesh,
        in_specs=(
            P(("wall", "drops"), None, None),
            P(("wall", "drops"), None, None),
            P(),
            P(("wall", "drops"), None, None),
            P(("wall", "drops"), None),
            P(("wall", "drops")),
            P("wall", None),
            P("wall", None),
            P(("wall", "drops"), None),
        ),
        out_specs=P(("wall", "drops"), None, None),
        check_vma=False,
    )
```

profile of v0, /device:TPU:11, one launch (start us, length us, event | category | flops | bytes accessed | tf_op | source)
XLA Modules:
  0.0 215.1 jit_solution(9322608203965364047)
XLA Ops:
  6.5 0.8 broadcast_in_dim.105
  7.3 0.6 broadcast_in_dim.106
  7.9 3.7 %all-to-all-start = ((s32[4,1,64]{2,1,0:T(1,128)}), s32[4,1,64]{2,1,0:T(1,128)S(1)}, u32[]{:S(2)}, u32[]{:S(2)}) async-start(s32[4,1,64]{2,1,0:T(1,128)} %broadcast_in_dim.106), calls=%async_computation | async-start | bytes 4096 | tf_op jit(solution)/shard_map/all_to_all | solution.py:189
  11.6 0.9 copy.22
  12.4 0.9 copy.23
  13.3 0.8 copy.21
  14.4 1.2 broadcast_in_dim.111
  15.5 6.5 %all-to-all-start.1 = ((f32[8,8,8,544]{3,2,1,0:T(8,128)}), f32[8,8,8,544]{3,2,1,0:T(8,128)}, u32[]{:S(2)}, u32[]{:S(2)}) async-start(f32[8,8,8,544]{3,2,1,0:T(8,128)} %broadcast_in_dim.111), calls=%async_computation.2 | async-start | bytes 2621440 | tf_op jit(solution)/shard_map/all_to_all | solution.py:181
  22.1 1.8 copy.19
  24.0 1.8 copy.20
  26.0 0.5 broadcast.216
  26.6 0.7 reduce.3
  27.3 2.6 %gather_fusion.1 = f32[256,192]{1,0:T(8,128)S(1)} fusion(f32[2048,192]{1,0:T(8,128)} %copy.19, s32[1024]{0:T(1024)S(1)} %pad_clamp_fusion.1), kind=kCustom, calls=%fused_computation.clone | custom fusion | bytes 394240 | tf_op jit(solution)/shard_map/jit(_take)/gather | solution.py:193
  29.9 1.0 gather_fusion.2
  30.9 0.1 broadcast_select_fusion.2
  31.0 0.9 maximum_select_fusion
  31.9 18.8 %all-to-all-done.1 = f32[8,8,8,544]{3,2,1,0:T(8,128)} async-done(((f32[8,8,8,544]{3,2,1,0:T(8,128)}), f32[8,8,8,544]{3,2,1,0:T(8,128)}, u32[]{:S(2)}, u32[]{:S(2)}) %all-to-all-start.1) | async-done | bytes 1114144 | tf_op jit(solution)/shard_map/all_to_all | solution.py:181
  50.7 1.9 gather_fusion
  52.6 0.1 broadcast_select_fusion.refs_1_
  52.8 5.3 %fusion.refs_0_ = f32[32,8,2112]{2,1,0:T(8,128)S(1)} fusion(f32[32,8,544]{2,1,0:T(8,128)S(1)} %broadcast_select_fusion.refs_1_, f32[544,2112]{1,0:T(8,128)} %param.13), kind=kOutput, calls=%fused_computation.3 | convolution fusion | flops 1764753408 | bytes 7315456 | tf_op jit(solution)/shard_map/dot_general | solution.py:198
  58.2 134.4 %shard_map.91.refs_4_ = f32[8,3,544]{2,1,0:T(4,128)S(1)} custom-call(s32[8]{0:T(128)S(1)} %copy-done, f32[32,8,2112]{2,1,0:T(8,128)S(1)} %fusion.refs_0_, f32[32,8,544]{2,1,0:T(8,128)S(1)} %broadcast_select_fusion.refs_1_, f32[8,2688]{1,0:T(8,128)S(1)} %select_select_fusion.refs_2_, f32[8,2688]{1,0:T(8,128)S(1)} %broadcast_in_dim.117.refs_3_, ...), custom_call_target="tpu_custom_call" | custom-call | flops 187170816000 | bytes 2752512 | tf_op jit(solution)/shard_map/pallas_call | solution.py:139
  192.6 1.0 reshape.171
  193.9 13.7 %shard_map.92 = f32[8,3,544]{2,1,0:T(4,128)S(1)} custom-call(s32[8]{0:T(128)S(1)} %broadcast_7_counts.2.counts, f32[8,8,512]{2,1,0:T(8,128)S(1)} %concatenate.11.refs_0_, f32[8,512]{1,0:T(8,128)S(1)} %select_select_fusion.1.refs_1_, f32[8,512]{1,0:T(8,128)S(1)} %broadcast_in_dim.122.refs_2_, f32[8,8,544]{2,1,0:T(8,128)S(1)} %maximum_maximum_fusion.refs_4_.refs_3_, ...), custom_call_target="tpu_custom_call" | custom-call | flops 8912896000 | bytes 131072 | tf_op jit(solution)/shard_map/pallas_call | solution.py:139
  207.6 0.6 copy.28
  (38 shorter events, 1.0 us)
Async XLA Ops:
  7.9 6.5 %all-to-all-start = ((s32[4,1,64]{2,1,0:T(1,128)}), s32[4,1,64]{2,1,0:T(1,128)S(1)}, u32[]{:S(2)}, u32[]{:S(2)}) async-start(s32[4,1,64]{2,1,0:T(1,128)} %broadcast_in_dim.106), calls=%async_computation | async-start | bytes 4096 | tf_op jit(solution)/shard_map/all_to_all | solution.py:189
  14.3 7.8 %copy-start.1 = (f32[2048,192]{0,1:T(8,128)S(1)}, f32[2048,192]{0,1:T(8,128)}, u32[]{:S(2)}) copy-start(f32[2048,192]{0,1:T(8,128)} %param.18) | copy-start | bytes 4718596
  14.4 43.7 %copy-start.3 = (f32[8]{0:T(128)}, f32[8]{0:T(128)S(1)}, u32[]{:S(2)}) copy-start(f32[8]{0:T(128)S(1)} %compare_convert_fusion) | copy-start | bytes 100
  15.5 35.2 %all-to-all-start.1 = ((f32[8,8,8,544]{3,2,1,0:T(8,128)}), f32[8,8,8,544]{3,2,1,0:T(8,128)}, u32[]{:S(2)}, u32[]{:S(2)}) async-start(f32[8,8,8,544]{3,2,1,0:T(8,128)} %broadcast_in_dim.111), calls=%async_computation.2 | async-start | bytes 2621440 | tf_op jit(solution)/shard_map/all_to_all | solution.py:181
  22.1 170.6 %reduce-scatter.2.cloned.1.call-start = ((), (), s32[]{:S(2)}) async-start(), calls=%async_computation.3 | async-start | bytes 491520 | tf_op jit(solution)/shard_map/reduce_scatter | solution.py:196
  24.0 1.8 copy-start.2
  52.7 5.4 %copy-start = (s32[8]{0:T(128)S(1)}, s32[8]{0:T(128)}, u32[]{:S(2)}) copy-start(s32[8]{0:T(128)} %counts.1) | copy-start | bytes 100
  58.2 135.6 %copy-start.4 = (f32[8]{0:T(128)S(1)}, f32[8]{0:T(128)}, u32[]{:S(2)}) copy-start(f32[8]{0:T(128)} %copy-done.3) | copy-start | bytes 100
Sparse Core Ops, SparseCore 0:
  32.0 24.4 reduce-scatter.1
where the time goes:
time: 218 us; the launch traced here: 215 us
  Pallas kernels  148 us (68%)
  waiting for transfers between devices  18.8 us (9%)
  local copies, waits for them, and re-layouts  16.9 us (8%)
  between operations  13.6 us (6%)
  starting transfers between devices  10.2 us (5%)
  matrix products  5.32 us (2%)
    pallas_call x2, Pallas kernels, pair_sums(): pl.pallas_call(functools.partial(pair_kernel, per_drop), out_shape=jax.Sh...  148 us
    all_to_all x1, waiting for transfers between devices, per_device(): lax.all_to_all(spread, 'drops', split_axis=0, concat_axis=0, tiled=True)  18.8 us
    all_to_all x1, starting transfers between devices, per_device(): lax.all_to_all(spread, 'drops', split_axis=0, concat_axis=0, tiled=True)  6.51 us
    unnamed x16, local copies, waits for them, and re-layouts  6.18 us
    dot_general x1, matrix products, per_device(): lax.dot_general(entries.reshape(-1, coarse), upsample, (((1,), (0,)), (()...  5.32 us
  transfers between devices with their start and end apart: 3, of which 1 were waited for; matrix products, arithmetic and copies ran while one was open for 9% of the time, Pallas kernels for 62%

commit v1 on v0

--- a/solution.py
+++ b/solution.py
@@ -32,16 +32,15 @@
 
 
 def pair_kernel(per_drop, counts, *refs):
-    count = len(refs) - 17
+    count = len(refs) - 15
     src, (scale, shift, tgt, base, out) = refs[:count], refs[count : count + 5]
     left, right, force, feat, acc_one, acc_cube = refs[count + 5 : count + 11]
-    dist, high, low = (refs[k : k + 2] for k in range(count + 11, count + 17, 2))
+    dist, split = refs[count + 11 : count + 13], refs[count + 13 :]
     width = scale.shape[1]
     row = lax.broadcasted_iota(jnp.int32, (8, width), 0)
 
     nodes = feat.shape[0]
     starts = list(range(0, width, CHUNK))
-    dims = (((1,), (1,)), ((), ()))
 
     def distances(n):
         size = min(CHUNK, width - starts[n])
@@ -58,23 +57,25 @@
         ]
         for top in range(0, nodes, GROUP):
             rows = slice(top, min(top + GROUP, nodes))
+            below = slice(nodes + rows.start, nodes + rows.stop)
             sums = [acc_one[c, rows] for c in range(3)]
             for weight, lane in zip(weights, lanes):
                 inverse = lax.rsqrt(dist[n % 2][rows, lane : lane + 128])
                 sums = [part + inverse * weight[c] for c, part in enumerate(sums)]
                 cubed = inverse * inverse * inverse
                 whole = cubed.astype(BF)
-                high[n % 2][rows, lane : lane + 128] = whole
-                low[n % 2][rows, lane : lane + 128] = (cubed - whole.astype(F32)).astype(BF)
+                split[n % 2][rows, lane : lane + 128] = whole
+                split[n % 2][below, lane : lane + 128] = (cubed - whole.astype(F32)).astype(BF)
             for c in range(3):
                 acc_one[c, rows] = sums[c]
 
     def sums(n):
         size = min(CHUNK, width - starts[n])
-        coefs = right[:, starts[n] : starts[n] + size]
-        acc_cube[...] += lax.dot_general(
-            high[n % 2][:, :size], coefs, dims, preferred_element_type=F32
-        ) + lax.dot_general(low[n % 2][:, :size], coefs, dims, preferred_element_type=F32)
+        acc_cube[...] += jnp.dot(
+            split[n % 2][:, :size],
+            right[starts[n] : starts[n] + size],
+            preferred_element_type=F32,
+        )
 
     def one_drop(i, _):
         acc_one[...] = jnp.zeros_like(acc_one)
@@ -99,12 +100,12 @@
             ).astype(BF)
             cross = [values * raw[3 + c : 4 + c] for c in range(3)]
             along = cross[0][0:1] + cross[1][1:2] + cross[2][2:3]
-            split = [kernel_pieces(part) for part in cross + [values * along]]
+            shares = [kernel_pieces(part) for part in cross + [values * along]]
             parts = []
             for p, whole in enumerate((first, second, third)):
-                parts += [whole] + [part[p] for part in split]
+                parts += [whole] + [part[p] for part in shares]
             parts.append(jnp.zeros_like(first))
-            right[...] = jnp.concatenate(parts, axis=0).astype(BF)
+            right[...] = jnp.concatenate(parts, axis=0).T.astype(BF)
 
             distances(0)
             for n in range(len(starts)):
@@ -116,7 +117,7 @@
 
         lax.fori_loop(0, counts[i], one_entry, 0)
 
-        turned = acc_cube[...].T
+        turned = (acc_cube[:nodes] + acc_cube[nodes:]).T
         cube = turned[0:40] + turned[40:80] + turned[80:120]
         plain = [jnp.sum(acc_one[c].T, axis=0, keepdims=True) for c in range(3)]
         x = 2.0 * own[3:6]
@@ -143,19 +144,28 @@
         out_specs=vmem,
         scratch_shapes=[
             pltpu.VMEM((64, width), BF),
-            pltpu.VMEM((128, width), BF),
+            pltpu.VMEM((width, 128), BF),
             pltpu.VMEM((8, width), F32),
             pltpu.VMEM((nodes, 64), BF),
             pltpu.VMEM((3, nodes, 128), F32),
-            pltpu.VMEM((nodes, 128), F32),
+            pltpu.VMEM((2 * nodes, 128), F32),
         ]
         + [pltpu.VMEM((nodes, CHUNK), F32)] * 2
-        + [pltpu.VMEM((nodes, CHUNK), BF)] * 4,
+        + [pltpu.VMEM((2 * nodes, CHUNK), BF)] * 2,
         compiler_params=pltpu.CompilerParams(vmem_limit_bytes=40 * 1024 * 1024),
         cost_estimate=pl.CostEstimate(
             flops=pairs * 4000, bytes_accessed=pairs // nodes * 32, transcendentals=pairs
         ),
     )(counts, *src, scale, shift, tgt, base)
+
+
+def scale_of(lanes, plus):
+    row = jnp.arange(8, dtype=jnp.int32)[:, None]
+    lane = jnp.arange(lanes, dtype=jnp.int32)[None, :]
+    sign = jnp.where((row < 3) & (lane >= plus), -2.0, 2.0)
+    return jnp.where(row < 6, sign, 0.0).astype(F32), jnp.broadcast_to(
+        (row == 6).astype(F32), (8, lanes)
+    )
 
 
 def per_device(
@@ -177,9 +187,10 @@
     packed = jnp.concatenate(
         [drop_strength, drop_points, jnp.zeros((owned, 2, coarse), F32)], axis=1
     )
-    spread = jnp.broadcast_to(packed[None], (group // owned,) + packed.shape)
+    flat = packed[:, :6].reshape(1, owned, 6 * coarse)
+    spread = jnp.broadcast_to(flat, (group // owned,) + flat.shape[1:])
     everyone = lax.all_to_all(spread, "drops", split_axis=0, concat_axis=0, tiled=True)
-    everyone = everyone.reshape(group, 8, coarse)
+    everyone = everyone.reshape(group, 6 * coarse)
 
     ranks = lax.axis_size("wall")
     held, patch_width = patch_points.shape
@@ -193,8 +204,20 @@
         [jnp.take(patch_strength, spot, axis=0), jnp.take(patch_points, spot, axis=0)], axis=1
     )
     reply = jnp.where(mine[:, None], reply, 0.0)
-    wall = lax.psum_scatter(reply, "wall", scatter_dimension=0, tiled=True)
-    entries = jnp.take(everyone, near_drops.reshape(-1) % group, axis=0)
+    reply = reply.reshape(ranks, owned * listed, 2 * patch_width)
+    back = lax.all_to_all(reply, "wall", split_axis=0, concat_axis=0, tiled=True)
+    wall = jnp.sum(back, axis=0)
+    wall = wall.reshape(owned, listed, 6, patch_nodes).transpose(0, 2, 1, 3)
+    wall = wall.reshape(owned, 6, listed * patch_nodes)
+    wall = jnp.concatenate([wall, jnp.zeros((owned, 2, listed * patch_nodes), F32)], axis=1)
+    wall_width = listed * patch_nodes
+    total = pair_sums(
+        jnp.ones((owned,), jnp.int32), (wall,), *scale_of(wall_width, wall_width), packed, base_velocity
+    )
+
+    everyone, total = lax.optimization_barrier((everyone, total))
+    entries = jnp.take(everyone, near_drops.reshape(-1) % group, axis=0).reshape(-1, 6, coarse)
+    entries = jnp.concatenate([entries, jnp.zeros((entries.shape[0], 2, coarse), F32)], axis=1)
     upsampled = lax.dot_general(
         entries.reshape(-1, coarse),
         upsample,
@@ -203,29 +226,7 @@
         preferred_element_type=F32,
     ).reshape(-1, 8, fine)
 
-    def scale_of(lanes, plus):
-        row = jnp.arange(8, dtype=jnp.int32)[:, None]
-        lane = jnp.arange(lanes, dtype=jnp.int32)[None, :]
-        sign = jnp.where((row < 3) & (lane >= plus), -2.0, 2.0)
-        return jnp.where(row < 6, sign, 0.0).astype(F32), jnp.broadcast_to(
-            (row == 6).astype(F32), (8, lanes)
-        )
-
-    near = pair_sums(
-        near_count, (upsampled, entries), *scale_of(width, fine), packed, base_velocity
-    )
-    wall, near = lax.optimization_barrier((wall, near))
-    wall = wall.reshape(owned, listed, 6, patch_nodes).transpose(0, 2, 1, 3)
-    wall = wall.reshape(owned, 6, listed * patch_nodes)
-    wall = jnp.concatenate([wall, jnp.zeros((owned, 2, listed * patch_nodes), F32)], axis=1)
-    wall_width = listed * patch_nodes
-    return pair_sums(
-        jnp.ones((owned,), jnp.int32),
-        (wall,),
-        *scale_of(wall_width, wall_width),
-        packed,
-        near,
-    )
+    return pair_sums(near_count, (upsampled, entries), *scale_of(width, fine), packed, total)
 
 
 def solution(mesh):

time: 218 us -> 196 us (0.90)
  between operations: 13.6 us -> 0.2 us
  waiting for transfers between devices: 18.8 us -> 9.25 us
  starting transfers between devices: 10.2 us -> 15 us
  Pallas kernels: 148 us -> 145 us
    all_to_all x1, waiting for transfers between devices: 18.8 us -> 4.82 us  [per_device(): lax.all_to_all(spread, 'drops', split_axis=0, concat_axis=0, tiled=True)]
    all_to_all x0 -> x1, waiting for transfers between devices: none -> 4.42 us  [per_device(): lax.all_to_all(reply, 'wall', split_axis=0, concat_axis=0, tiled=True)]
    all_to_all x0 -> x1, starting transfers between devices: none -> 3.63 us  [per_device(): lax.all_to_all(reply, 'wall', split_axis=0, concat_axis=0, tiled=True)]
    pallas_call x2, Pallas kernels: 148 us -> 145 us  [pair_sums(): pl.pallas_call(functools.partial(pair_kernel, per_drop), out_shape=jax.Sh...]
    unnamed x16 -> x10, local copies, waits for them, and re-layouts: 6.18 us -> 7.18 us
  transfers between devices with their start and end apart: 3 -> 3, of which waited for: 1 -> 2; matrix products, arithmetic and copies ran while one was open for 9% -> 5% of each run, Pallas kernels for 62% -> 7%
where the time goes in v1:
time: 196 us; the launch traced here: 194 us
  Pallas kernels  145 us (74%)
  local copies, waits for them, and re-layouts  16 us (8%)
  starting transfers between devices  15 us (8%)
  waiting for transfers between devices  9.25 us (5%)
  matrix products  5.33 us (3%)
  other arithmetic  3.02 us (2%)
    pallas_call x2, Pallas kernels, pair_sums(): pl.pallas_call(functools.partial(pair_kernel, per_drop), out_shape=jax.Sh...  145 us
    all_to_all x1, starting transfers between devices, per_device(): lax.all_to_all(spread, 'drops', split_axis=0, concat_axis=0, tiled=True)  7.7 us
    unnamed x10, local copies, waits for them, and re-layouts  7.18 us
    dot_general x1, matrix products, per_device(): lax.dot_general(entries.reshape(-1, coarse), upsample, (((1,), (0,)), (()...  5.33 us
    all_to_all x1, waiting for transfers between devices, per_device(): lax.all_to_all(spread, 'drops', split_axis=0, concat_axis=0, tiled=True)  4.82 us
    all_to_all x1, waiting for transfers between devices, per_device(): lax.all_to_all(reply, 'wall', split_axis=0, concat_axis=0, tiled=True)  4.42 us
  transfers between devices with their start and end apart: 3, of which 2 were waited for; matrix products, arithmetic and copies ran while one was open for 5% of the time, Pallas kernels for 7%

profile of v1, /device:TPU:11, one launch (start us, length us, event | category | flops | bytes accessed | tf_op | source)
XLA Modules:
  0.0 194.3 jit_solution(8202563787369060359)
XLA Ops:
  0.0 0.8 broadcast_in_dim.110
  0.8 0.6 broadcast_in_dim.111
  1.4 3.7 %all-to-all-start.1 = ((s32[4,1,64]{2,1,0:T(1,128)}), s32[4,1,64]{2,1,0:T(1,128)S(1)}, u32[]{:S(2)}, u32[]{:S(2)}) async-start(s32[4,1,64]{2,1,0:T(1,128)} %broadcast_in_dim.111), calls=%async_computation.1 | async-start | bytes 4096 | tf_op jit(solution)/shard_map/all_to_all | solution.py:200
  5.1 0.9 copy.35
  5.9 0.9 copy.36
  6.8 0.9 pad_maximum_fusion
  7.6 0.8 copy.29
  8.7 2.8 %copy.31 = f32[2048,192]{1,0:T(8,128)} copy(f32[2048,192]{0,1:T(8,128)} %param.18) | data formatting | bytes 3145728 | tf_op args[7]
  11.5 1.8 copy.32
  13.6 0.5 broadcast.206
  14.2 0.7 reduce.3
  14.9 2.6 %gather_fusion.1 = f32[256,192]{1,0:T(8,128)S(1)} fusion(f32[2048,192]{1,0:T(8,128)} %copy.31, s32[1024]{0:T(1024)S(1)} %pad_clamp_fusion.1), kind=kCustom, calls=%fused_computation.clone | custom fusion | bytes 394240 | tf_op jit(solution)/shard_map/jit(_take)/gather | solution.py:204
  17.5 1.0 gather_fusion.2
  18.6 0.9 maximum_select_fusion
  19.5 3.6 %all-to-all-start.2 = ((f32[4,64,384]{2,1,0:T(8,128)}), f32[4,64,384]{2,1,0:T(8,128)S(1)}, u32[]{:S(2)}, u32[]{:S(2)}) async-start(f32[4,64,384]{2,1,0:T(8,128)} %maximum_select_fusion), calls=%async_computation.2 | async-start | bytes 786432 | tf_op jit(solution)/shard_map/all_to_all | solution.py:208
  23.2 4.4 %all-to-all-done.2 = f32[4,64,384]{2,1,0:T(8,128)S(1)} async-done(((f32[4,64,384]{2,1,0:T(8,128)}), f32[4,64,384]{2,1,0:T(8,128)S(1)}, u32[]{:S(2)}, u32[]{:S(2)}) %all-to-all-start.2) | async-done | bytes 393248 | tf_op jit(solution)/shard_map/all_to_all | solution.py:208
  27.7 1.0 broadcast_in_dim.109
  28.6 7.7 %all-to-all-start = ((f32[8,8,3264]{2,1,0:T(8,128)}), f32[8,8,3264]{2,1,0:T(8,128)S(1)}, u32[]{:S(2)}, u32[]{:S(2)}) async-start(f32[8,8,3264]{2,1,0:T(8,128)} %broadcast_in_dim.109), calls=%async_computation | async-start | bytes 1703936 | tf_op jit(solution)/shard_map/all_to_all | solution.py:192
  36.8 13.5 %shard_map.91.refs_5_ = f32[8,3,544]{2,1,0:T(4,128)S(1)} custom-call(s32[8]{0:T(128)S(1)} %broadcast_9_counts.2.counts, f32[8,8,512]{2,1,0:T(8,128)S(1)} %concatenate.24.refs_0_, f32[8,512]{1,0:T(8,128)S(1)} %select_select_fusion.1.refs_1_, f32[8,512]{1,0:T(8,128)S(1)} %broadcast_in_dim.118.refs_2_, f32[8,8,544]{2,1,0:T(8,128)S(1)} %maximum_maximum_fusion.refs_3_.refs_4_, ...), custom_call_target="tpu_custom_call" | custom-call | flops 8912896000 | bytes 131072 | tf_op jit(solution)/shard_map/pallas_call | solution.py:140
  50.3 4.8 %all-to-all-done = f32[8,8,3264]{2,1,0:T(8,128)S(1)} async-done(((f32[8,8,3264]{2,1,0:T(8,128)}), f32[8,8,3264]{2,1,0:T(8,128)S(1)}, u32[]{:S(2)}, u32[]{:S(2)}) %all-to-all-start) | async-done | bytes 835616 | tf_op jit(solution)/shard_map/all_to_all | solution.py:192
  55.1 0.7 gather_fusion
  56.3 5.3 %fusion.refs_0_ = f32[32,8,2112]{2,1,0:T(8,128)S(1)} fusion(f32[544,2112]{1,0:T(8,128)} %param.13, f32[32,6,544]{2,1,0:T(8,128)S(1)} %broadcast_select_fusion), kind=kOutput, calls=%fused_computation.3 | convolution fusion | flops 1764753408 | bytes 7176192 | tf_op jit(solution)/shard_map/dot_general | solution.py:221
  61.7 132.0 %shard_map.92 = f32[8,3,544]{2,1,0:T(4,128)S(1)} custom-call(s32[8]{0:T(128)S(1)} %copy-done, f32[32,8,2112]{2,1,0:T(8,128)S(1)} %fusion.refs_0_, f32[32,8,544]{2,1,0:T(8,128)S(1)} %concatenate.26.refs_1_, f32[8,2688]{1,0:T(8,128)S(1)} %select_select_fusion.refs_2_, f32[8,2688]{1,0:T(8,128)S(1)} %broadcast_in_dim.125.refs_3_, ...), custom_call_target="tpu_custom_call" | custom-call | flops 187170816000 | bytes 2752512 | tf_op jit(solution)/shard_map/pallas_call | solution.py:140
  193.7 0.6 copy.39
  (38 shorter events, 1.8 us)
Async XLA Ops:
  1.4 12.3 %all-to-all-start.1 = ((s32[4,1,64]{2,1,0:T(1,128)}), s32[4,1,64]{2,1,0:T(1,128)S(1)}, u32[]{:S(2)}, u32[]{:S(2)}) async-start(s32[4,1,64]{2,1,0:T(1,128)} %broadcast_in_dim.111), calls=%async_computation.1 | async-start | bytes 4096 | tf_op jit(solution)/shard_map/all_to_all | solution.py:200
  11.5 1.8 copy-start.1
  19.5 8.1 %all-to-all-start.2 = ((f32[4,64,384]{2,1,0:T(8,128)}), f32[4,64,384]{2,1,0:T(8,128)S(1)}, u32[]{:S(2)}, u32[]{:S(2)}) async-start(f32[4,64,384]{2,1,0:T(8,128)} %maximum_select_fusion), calls=%async_computation.2 | async-start | bytes 786432 | tf_op jit(solution)/shard_map/all_to_all | solution.py:208
  28.6 26.5 %all-to-all-start = ((f32[8,8,3264]{2,1,0:T(8,128)}), f32[8,8,3264]{2,1,0:T(8,128)S(1)}, u32[]{:S(2)}, u32[]{:S(2)}) async-start(f32[8,8,3264]{2,1,0:T(8,128)} %broadcast_in_dim.109), calls=%async_computation | async-start | bytes 1703936 | tf_op jit(solution)/shard_map/all_to_all | solution.py:192
  56.3 5.4 %copy-start = (s32[8]{0:T(128)S(1)}, s32[8]{0:T(128)}, u32[]{:S(2)}) copy-start(s32[8]{0:T(128)} %counts.1) | copy-start | bytes 100

commit v2 on v1

--- a/solution.py
+++ b/solution.py
@@ -8,7 +8,7 @@
 from jax.sharding import PartitionSpec as P
 
 BF, F32 = jnp.bfloat16, jnp.float32
-CHUNK = 512
+CHUNK = 1024
 GROUP = 16
 
 

time: 196 us -> 201 us (1.026)
  the two profiles are of different devices: /device:TPU:11 before, /device:TPU:0 now
where the time goes in v2:
time: 201 us; the launch traced here: 200 us
  Pallas kernels  148 us (74%)
  local copies, waits for them, and re-layouts  16 us (8%)
  starting transfers between devices  14.2 us (7%)
  waiting for transfers between devices  13.9 us (7%)
  matrix products  5.32 us (3%)
  other arithmetic  3.02 us (2%)
    pallas_call x2, Pallas kernels, pair_sums(): pl.pallas_call(functools.partial(pair_kernel, per_drop), out_shape=jax.Sh...  148 us
    all_to_all x1, waiting for transfers between devices, per_device(): lax.all_to_all(spread, 'drops', split_axis=0, concat_axis=0, tiled=True)  7.97 us
    unnamed x10, local copies, waits for them, and re-layouts  7.18 us
    all_to_all x1, waiting for transfers between devices, per_device(): lax.all_to_all(reply, 'wall', split_axis=0, concat_axis=0, tiled=True)  5.92 us
    dot_general x1, matrix products, per_device(): lax.dot_general(entries.reshape(-1, coarse), upsample, (((1,), (0,)), (()...  5.32 us
    all_to_all x1, starting transfers between devices, per_device(): lax.all_to_all(lists, 'wall', split_axis=0, concat_axis=0, tiled=True)  5.16 us
    all_to_all x1, starting transfers between devices, per_device(): lax.all_to_all(spread, 'drops', split_axis=0, concat_axis=0, tiled=True)  4.88 us
    all_to_all x1, starting transfers between devices, per_device(): lax.all_to_all(reply, 'wall', split_axis=0, concat_axis=0, tiled=True)  4.19 us
  transfers between devices with their start and end apart: 3, of which 2 were waited for; matrix products, arithmetic and copies ran while one was open for 5% of the time, Pallas kernels for 7%

profile of v2, /device:TPU:0, one launch (start us, length us, event | category | flops | bytes accessed | tf_op | source)
XLA Modules:
  0.0 200.3 jit_solution(8586379387957927410)
XLA Ops:
  0.0 0.8 broadcast_in_dim.110
  0.8 0.6 broadcast_in_dim.111
  1.4 5.2 %all-to-all-start.1 = ((s32[4,1,64]{2,1,0:T(1,128)}), s32[4,1,64]{2,1,0:T(1,128)S(1)}, u32[]{:S(2)}, u32[]{:S(2)}) async-start(s32[4,1,64]{2,1,0:T(1,128)} %broadcast_in_dim.111), calls=%async_computation.1 | async-start | bytes 4096 | tf_op jit(solution)/shard_map/all_to_all | solution.py:200
  6.5 0.9 copy.35
  7.4 0.9 copy.36
  8.2 0.9 pad_maximum_fusion
  9.1 0.8 copy.29
  10.2 2.8 %copy.31 = f32[2048,192]{1,0:T(8,128)} copy(f32[2048,192]{0,1:T(8,128)} %param.18) | data formatting | bytes 3145728 | tf_op args[7]
  13.0 1.8 copy.32
  15.1 0.5 broadcast.206
  15.6 0.7 reduce.3
  16.4 2.6 %gather_fusion.1 = f32[256,192]{1,0:T(8,128)S(1)} fusion(f32[2048,192]{1,0:T(8,128)} %copy.31, s32[1024]{0:T(1024)S(1)} %pad_clamp_fusion.1), kind=kCustom, calls=%fused_computation.clone | custom fusion | bytes 394240 | tf_op jit(solution)/shard_map/jit(_take)/gather | solution.py:204
  19.0 1.0 gather_fusion.2
  20.1 0.9 maximum_select_fusion
  21.0 4.2 %all-to-all-start.2 = ((f32[4,64,384]{2,1,0:T(8,128)}), f32[4,64,384]{2,1,0:T(8,128)S(1)}, u32[]{:S(2)}, u32[]{:S(2)}) async-start(f32[4,64,384]{2,1,0:T(8,128)} %maximum_select_fusion), calls=%async_computation.2 | async-start | bytes 786432 | tf_op jit(solution)/shard_map/all_to_all | solution.py:208
  25.3 5.9 %all-to-all-done.2 = f32[4,64,384]{2,1,0:T(8,128)S(1)} async-done(((f32[4,64,384]{2,1,0:T(8,128)}), f32[4,64,384]{2,1,0:T(8,128)S(1)}, u32[]{:S(2)}, u32[]{:S(2)}) %all-to-all-start.2) | async-done | bytes 393248 | tf_op jit(solution)/shard_map/all_to_all | solution.py:208
  31.2 1.0 broadcast_in_dim.109
  32.1 4.9 %all-to-all-start = ((f32[8,8,3264]{2,1,0:T(8,128)}), f32[8,8,3264]{2,1,0:T(8,128)S(1)}, u32[]{:S(2)}, u32[]{:S(2)}) async-start(f32[8,8,3264]{2,1,0:T(8,128)} %broadcast_in_dim.109), calls=%async_computation | async-start | bytes 1703936 | tf_op jit(solution)/shard_map/all_to_all | solution.py:192
  37.5 13.9 %shard_map.91.refs_5_ = f32[8,3,544]{2,1,0:T(4,128)S(1)} custom-call(s32[8]{0:T(128)S(1)} %broadcast_9_counts.2.counts, f32[8,8,512]{2,1,0:T(8,128)S(1)} %concatenate.24.refs_0_, f32[8,512]{1,0:T(8,128)S(1)} %select_select_fusion.1.refs_1_, f32[8,512]{1,0:T(8,128)S(1)} %broadcast_in_dim.118.refs_2_, f32[8,8,544]{2,1,0:T(8,128)S(1)} %maximum_maximum_fusion.refs_3_.refs_4_, ...), custom_call_target="tpu_custom_call" | custom-call | flops 8912896000 | bytes 131072 | tf_op jit(solution)/shard_map/pallas_call | solution.py:140
  51.4 8.0 %all-to-all-done = f32[8,8,3264]{2,1,0:T(8,128)S(1)} async-done(((f32[8,8,3264]{2,1,0:T(8,128)}), f32[8,8,3264]{2,1,0:T(8,128)S(1)}, u32[]{:S(2)}, u32[]{:S(2)}) %all-to-all-start) | async-done | bytes 835616 | tf_op jit(solution)/shard_map/all_to_all | solution.py:192
  59.4 0.7 gather_fusion
  60.6 5.3 %fusion.refs_0_ = f32[32,8,2112]{2,1,0:T(8,128)S(1)} fusion(f32[544,2112]{1,0:T(8,128)} %param.13, f32[32,6,544]{2,1,0:T(8,128)S(1)} %broadcast_select_fusion), kind=kOutput, calls=%fused_computation.3 | convolution fusion | flops 1764753408 | bytes 7176192 | tf_op jit(solution)/shard_map/dot_general | solution.py:221
  66.0 133.7 %shard_map.92 = f32[8,3,544]{2,1,0:T(4,128)S(1)} custom-call(s32[8]{0:T(128)S(1)} %copy-done, f32[32,8,2112]{2,1,0:T(8,128)S(1)} %fusion.refs_0_, f32[32,8,544]{2,1,0:T(8,128)S(1)} %concatenate.26.refs_1_, f32[8,2688]{1,0:T(8,128)S(1)} %select_select_fusion.refs_2_, f32[8,2688]{1,0:T(8,128)S(1)} %broadcast_in_dim.125.refs_3_, ...), custom_call_target="tpu_custom_call" | custom-call | flops 187170816000 | bytes 2752512 | tf_op jit(solution)/shard_map/pallas_call | solution.py:140
  199.7 0.6 copy.39
  (38 shorter events, 1.8 us)
Async XLA Ops:
  1.4 13.8 %all-to-all-start.1 = ((s32[4,1,64]{2,1,0:T(1,128)}), s32[4,1,64]{2,1,0:T(1,128)S(1)}, u32[]{:S(2)}, u32[]{:S(2)}) async-start(s32[4,1,64]{2,1,0:T(1,128)} %broadcast_in_dim.111), calls=%async_computation.1 | async-start | bytes 4096 | tf_op jit(solution)/shard_map/all_to_all | solution.py:200
  13.0 1.8 copy-start.1
  21.0 10.2 %all-to-all-start.2 = ((f32[4,64,384]{2,1,0:T(8,128)}), f32[4,64,384]{2,1,0:T(8,128)S(1)}, u32[]{:S(2)}, u32[]{:S(2)}) async-start(f32[4,64,384]{2,1,0:T(8,128)} %maximum_select_fusion), calls=%async_computation.2 | async-start | bytes 786432 | tf_op jit(solution)/shard_map/all_to_all | solution.py:208
  32.1 27.3 %all-to-all-start = ((f32[8,8,3264]{2,1,0:T(8,128)}), f32[8,8,3264]{2,1,0:T(8,128)S(1)}, u32[]{:S(2)}, u32[]{:S(2)}) async-start(f32[8,8,3264]{2,1,0:T(8,128)} %broadcast_in_dim.109), calls=%async_computation | async-start | bytes 1703936 | tf_op jit(solution)/shard_map/all_to_all | solution.py:192
  60.6 5.4 %copy-start = (s32[8]{0:T(128)S(1)}, s32[8]{0:T(128)}, u32[]{:S(2)}) copy-start(s32[8]{0:T(128)} %counts.1) | copy-start | bytes 100
